TPU v7x, 32 devices: a whole 2x2x4 slice. The times are simulated.
32 devices in a mesh: trial: 2 (over y), ha: 4 (over z), wa: 4 (over x, core).
Axes of the slice: x: 2, y: 2, z: 4, core: 2. Of those that a mesh axis runs over, the one named last changes fastest.
Arguments:
- volume: bfloat16 [32, 256, 512], P(('trial', 'ha'), 'wa'), parts along dimension 0, may hold values from -6 to 6
- grad_out: bfloat16 [32, 256, 512], P(('trial', 'ha'), 'wa'), parts along dimension 0, may hold values from -12 to 12
- filter_one: float32 [27, 1024], replicated, may hold values from -4 to 4
- filter_two: float32 [27, 1024], replicated, may hold values from -4 to 4
- step_size: float32 [2], P('trial'), parts along dimension 0, may hold values from 0.05 to 0.5
Outputs:
- grad_input: bfloat16 [32, 256, 512], P(('trial', 'ha'), 'wa'), parts along dimension 0
- new_one: float32 [54, 1024], P('trial'), parts along dimension 0
- new_two: float32 [54, 1024], P('trial'), parts along dimension 0
There are 2 independent parts, one for each index of `trial`. A program takes and returns all parts, laid end to end along the dimension named above; an argument that names none is the same for every part. Nothing has to cross between parts.
All inputs are finite; a program needn't handle non-finite values.
Results may differ from a plain program's by a relative error of at most 0.0024.
The roundings to bfloat16 on the way count: a program that leaves them out, or rounds other values in their place, can miss the bound.
Values may be sent and summed in bfloat16 or wider, within the bound.
A program may use at most 128 MiB of HBM per device.

v0:
```python
import functools
import math

import jax
import jax.numpy as jnp
from jax import lax
from jax.experimental import pallas as pl
from jax.experimental.pallas import tpu as pltpu
from jax.sharding import PartitionSpec as P

C = 32
SLOPE = 0.1
LOG2 = math.log(2.0)
MESH = pl.DeviceIdType.MESH
SIDES = ((-1, 0), (1, 0), (0, -1), (0, 1), (-1, -1), (-1, 1), (1, -1), (1, 1))
OPPOSITE = (1, 0, 3, 2, 7, 6, 5, 4)


def kernel(
    high, wide, v_ref, g_ref, k_ref, out_ref, sums_ref,
    band, px, own, edge, row_in, edge_in, slope_one, gt, send_sem, recv_sem,
):
    rows, cols, lanes = v_ref.shape
    cells = rows * cols
    tiles = lanes // 128
    ih, iw = lax.axis_index("ha"), lax.axis_index("wa")
    f32, bf16 = jnp.float32, jnp.bfloat16

    def has(d):
        dh, dw = SIDES[d]
        ok = None
        for step, at, count in ((dh, ih, high), (dw, iw, wide)):
            if step:
                one = (at > 0) if step < 0 else (at < count - 1)
                ok = one if ok is None else jnp.logical_and(ok, one)
        return ok

    def target(d):
        return {"ha": ih + SIDES[d][0], "wa": iw + SIDES[d][1]}

    def landing(k, d):
        return row_in.at[k, d] if d < 2 else edge_in.at[k, d - 2]

    def copy_of(k, d):
        if d < 2:
            at = 0 if d == 0 else rows - 1
            source = v_ref.at[at] if k == 0 else own.at[k - 1, at]
        else:
            source = edge.at[k, 0 if SIDES[d][1] < 0 else 1]
        return pltpu.make_async_remote_copy(
            src_ref=source,
            dst_ref=landing(k, OPPOSITE[d]),
            send_sem=send_sem.at[k, d],
            recv_sem=recv_sem.at[k, OPPOSITE[d]],
            device_id=target(d),
            device_id_type=MESH,
        )

    def arrival_of(k, d):
        return pltpu.make_async_remote_copy(
            src_ref=landing(k, d),
            dst_ref=landing(k, d),
            send_sem=send_sem.at[k, d],
            recv_sem=recv_sem.at[k, d],
            device_id=target(d),
            device_id_type=MESH,
        )

    def set_edges(k, value):
        for r in range(rows):
            edge[k, 0, r : r + 1, :] = value[r, 0:1, :]
            edge[k, 1, r : r + 1, :] = value[r, cols - 1 : cols, :]

    def send(k):
        for d in range(8):
            @pl.when(has(d))
            def _():
                copy_of(k, d).start()

    def receive(k):
        for d in range(8):
            @pl.when(has(d))
            def _():
                arrival_of(k, d).wait_recv()

    def finish():
        for k in range(4):
            for d in range(8):
                @pl.when(has(d))
                def _():
                    copy_of(k, d).wait_send()

    col = lax.broadcasted_iota(jnp.int32, (cols, lanes), 0)

    def put_row(k, r, value, left, right):
        px[k, r, :, 0:lanes] = jnp.where(col == 0, left, pltpu.roll(value, 1, 0)).astype(bf16)
        px[k, r, :, lanes : 2 * lanes] = value.astype(bf16)
        px[k, r, :, 2 * lanes :] = jnp.where(
            col == cols - 1, right, pltpu.roll(value, cols - 1, 0)
        ).astype(bf16)

    def assemble(k, value):
        last = rows - 1
        for r in range(rows):
            put_row(k, r + 1, value[r], edge_in[k, 0, r : r + 1, :], edge_in[k, 1, r : r + 1, :])
        put_row(k, 0, row_in[k, 0].astype(f32),
                edge_in[k, 2, last : last + 1, :], edge_in[k, 3, last : last + 1, :])
        put_row(k, rows + 1, row_in[k, 1].astype(f32),
                edge_in[k, 4, 0:1, :], edge_in[k, 5, 0:1, :])

    def conv(k, f):
        total = jnp.zeros((cells, lanes), f32)
        for a in range(3):
            left = px[k, a : a + rows].reshape(cells, 3 * lanes)
            total += jnp.dot(left, band[f, a], preferred_element_type=f32)
        return total

    def conv_back(k, f):
        total = jnp.zeros((cells, lanes), f32)
        for a in range(3):
            for b in range(3):
                left = px[k, a : a + rows, :, b * lanes : (b + 1) * lanes].reshape(cells, lanes)
                right = band[f, 2 - a, (2 - b) * lanes : (3 - b) * lanes, :]
                total += lax.dot_general(
                    left, right, (((1,), (1,)), ((), ())), preferred_element_type=f32
                )
        return total

    def filter_sums(k, f, grad):
        gt[C : C + lanes, :] = grad.T.astype(bf16)
        group = lax.broadcasted_iota(jnp.int32, (C, 128), 1) // C
        for a in range(3):
            total = jnp.zeros((6 * C, 384), f32)
            for q in range(tiles):
                source = jnp.concatenate(
                    [
                        px[k, a : a + rows, :, b * lanes + q * 128 : b * lanes + (q + 1) * 128]
                        .reshape(cells, 128)
                        for b in range(3)
                    ],
                    axis=1,
                )
                total += jnp.dot(
                    gt[q * 128 : q * 128 + 6 * C, :], source, preferred_element_type=f32
                )
            for c in range(3):
                result = jnp.zeros((C, 128), f32)
                for b in range(3):
                    part = jnp.zeros((C, 128), f32)
                    for s in range(4):
                        at = (s + 2 - c) * C
                        block = total[at : at + C, b * 128 : (b + 1) * 128]
                        part = jnp.where(group == s, block, part)
                    part = part + pltpu.roll(part, 64, 1)
                    part = part + pltpu.roll(part, 32, 1)
                    result = jnp.where(group == b, part, result)
                sums_ref[f, a, c * C : (c + 1) * C, :] = result

    def build(f):
        lane = lax.broadcasted_iota(jnp.int32, (C, 128), 1)
        zero = jnp.zeros((C, 128), f32)
        for a in range(3):
            for b in range(3):
                strip = k_ref[f, a * 3 + b].astype(f32)
                turned = [
                    pltpu.roll(strip, 96, 1), strip, pltpu.roll(strip, 32, 1), pltpu.roll(strip, 64, 1)
                ]
                for s in range(4):
                    turn = turned[s]
                    low = high_part = zero
                    middle = turn
                    if s == 0:
                        middle = jnp.where(lane < 64, turn, 0.0)
                        low = jnp.where(lane >= 96, turn, 0.0)
                    if s == 3:
                        middle = jnp.where(lane >= 64, turn, 0.0)
                        high_part = jnp.where(lane < 32, turn, 0.0)
                    low, middle, high_part, none = (
                        x.astype(bf16) for x in (low, middle, high_part, zero)
                    )
                    for q in range(tiles):
                        at = b * lanes + q * 128 + s * C
                        for t in range(tiles):
                            block = {-1: low, 0: middle, 1: high_part}.get(t - q, none)
                            band[f, a, at : at + C, t * 128 : (t + 1) * 128] = block

    def sharing(values):
        small = jnp.exp(-jnp.abs(values))
        share = 1.0 / (1.0 + small)
        return small, SLOPE + (1.0 - SLOPE) * jnp.where(values >= 0, share, small * share)

    barrier = pltpu.get_barrier_semaphore()
    for d in range(8):
        @pl.when(has(d))
        def _():
            pl.semaphore_signal(barrier, inc=1, device_id=target(d), device_id_type=MESH)

    edge[...] = jnp.zeros(edge.shape, f32)
    gt[...] = jnp.zeros(gt.shape, bf16)
    for d in range(8):
        @pl.when(jnp.logical_not(has(d)))
        def _():
            for k in range(4):
                if d < 2:
                    row_in[k, d] = jnp.zeros((cols, lanes), bf16)
                else:
                    edge_in[k, d - 2] = jnp.zeros(edge.shape[2:], f32)
    volume = v_ref[...].astype(f32)
    set_edges(0, volume)
    tall = 1 + jnp.where(ih > 0, 1, 0) + jnp.where(ih < high - 1, 1, 0)
    broad = 1 + jnp.where(iw > 0, 1, 0) + jnp.where(iw < wide - 1, 1, 0)
    pl.semaphore_wait(barrier, tall * broad - 1)
    send(0)
    build(0)
    build(1)
    receive(0)
    assemble(0, v_ref[...].astype(f32))

    hidden = conv(0, 0)
    small, slope = sharing(hidden)
    slope_one[...] = slope
    soft = jnp.maximum(hidden, 0.0) + jnp.log(1.0 + small)
    act = (SLOPE * hidden + (1.0 - SLOPE) * (soft - LOG2)).astype(bf16).reshape(rows, cols, lanes)
    own[0] = act
    set_edges(1, act.astype(f32))
    send(1)
    receive(1)
    assemble(1, own[0].astype(f32))

    slope = sharing(conv(1, 1))[1]
    grad = (g_ref[...].astype(f32).reshape(cells, lanes) * slope).astype(bf16)
    own[1] = grad.reshape(rows, cols, lanes)
    set_edges(2, own[1].astype(f32))
    send(2)
    filter_sums(1, 1, own[1].astype(f32).reshape(cells, lanes))
    receive(2)
    assemble(2, own[1].astype(f32))

    grad = (conv_back(2, 1) * slope_one[...]).astype(bf16)
    own[2] = grad.reshape(rows, cols, lanes)
    set_edges(3, own[2].astype(f32))
    send(3)
    filter_sums(0, 0, own[2].astype(f32).reshape(cells, lanes))
    receive(3)
    assemble(3, own[2].astype(f32))

    out_ref[...] = conv_back(3, 0).astype(bf16).reshape(rows, cols, lanes)
    finish()


def strips(kernel_one):
    parts = kernel_one.reshape(9, 3, C, C)[:, ::-1].transpose(0, 2, 1, 3).reshape(9, C, 3 * C)
    return jnp.pad(parts, ((0, 0), (0, 0), (0, C)))


def per_device(volume, grad_out, filter_one, filter_two, step_size):
    scale = 1.0 / math.sqrt(27.0 * C)
    kernels = jnp.stack(
        [strips((f * scale).astype(jnp.bfloat16)) for f in (filter_one, filter_two)]
    )
    rows, cols, lanes = volume.shape
    tall = -(-rows // 8) * 8
    vmem = pl.BlockSpec(memory_space=pltpu.VMEM)
    grad_input, sums = pl.pallas_call(
        functools.partial(kernel, lax.axis_size("ha"), lax.axis_size("wa")),
        out_shape=(
            jax.ShapeDtypeStruct(volume.shape, jnp.bfloat16),
            jax.ShapeDtypeStruct((2, 3, 3 * C, 128), jnp.float32),
        ),
        in_specs=[vmem] * 3,
        out_specs=(vmem, vmem),
        scratch_shapes=[
            pltpu.VMEM((2, 3, 3 * lanes, lanes), jnp.bfloat16),
            pltpu.VMEM((4, rows + 2, cols, 3 * lanes), jnp.bfloat16),
            pltpu.VMEM((3, rows, cols, lanes), jnp.bfloat16),
            pltpu.VMEM((4, 2, tall, lanes), jnp.float32),
            pltpu.VMEM((4, 2, cols, lanes), jnp.bfloat16),
            pltpu.VMEM((4, 6, tall, lanes), jnp.float32),
            pltpu.VMEM((rows * cols, lanes), jnp.float32),
            pltpu.VMEM((lanes + 2 * C, rows * cols), jnp.bfloat16),
            pltpu.SemaphoreType.DMA((4, 8)),
            pltpu.SemaphoreType.DMA((4, 8)),
        ],
        compiler_params=pltpu.CompilerParams(
            collective_id=0, has_side_effects=True, vmem_limit_bytes=44 * 2**20
        ),
    )(volume, grad_out, kernels)
    totals = lax.psum(sums, ("ha", "wa"))
    totals = (
        totals.reshape(2, 3, 3, C, 4, C)[:, :, :, :, :3]
        .transpose(0, 1, 4, 2, 5, 3)
        .reshape(2, 27, C * C)
    )
    filters = jnp.stack([filter_one, filter_two])
    spread = jnp.sqrt(jnp.mean(totals * totals, axis=(1, 2)) + 1e-06)
    result = filters - step_size[0] * totals / spread[:, None, None]
    return (grad_input, result[0], result[1])


def solution(mesh):
    placed = (P(("trial", "ha"), "wa", None), P(("trial", "ha"), "wa", None), P(), P(), P("trial"))
    return jax.shard_map(
        per_device,
        mesh=mesh,
        in_specs=placed,
        out_specs=(P(("trial", "ha"), "wa", None), P("trial", None), P("trial", None)),
        check_vma=False,
    )
```

profile of v0, /device:TPU:0, one launch (start us, length us, event | category | flops | bytes accessed | tf_op | source)
XLA Modules:
  0.0 145.0 jit_solution(5033928997103253235)
XLA Ops:
  7.2 0.0 all-reduce.4.cloned.1.call-start
  7.2 0.9 multiply_convert_fusion
  8.2 0.2 reshape.31
  8.4 0.2 copy.12
  8.5 1.0 rev.7
  9.5 0.2 reshape.32
  9.7 0.2 reshape.29
  9.9 0.2 copy.11
  10.1 1.0 rev.6
  11.1 0.2 reshape.30
  11.3 27.2 %shard_map.76 = (bf16[4,64,512]{2,1,0:T(8,128)(2,1)S(1)}, f32[2,3,96,128]{3,2,1,0:T(8,128)S(1)}) custom-call(bf16[4,64,512]{2,1,0:T(8,128)(2,1)S(1)} %copy-done, bf16[4,64,512]{2,1,0:T(8,128)(2,1)S(1)} %copy-done.1, bf16[2,9,32,128]{3,2,1,0:T(8,128)(2,1)S(1)} %pad_maximum_fusion.k_ref), custom_call_target="tpu_custom_call" | custom-call | tf_op jit(solution)/shard_map/pallas_call | solution.py:264
  38.5 0.5 reshape.33
  39.0 1.4 copy.13
  40.4 0.9 copy-done.2
  41.3 0.1 stack.22
  41.4 0.1 stack.21
  42.1 91.6 %all-reduce.4.cloned.1.call-done = f32[2,3,3,32,4,32]{3,5,0,2,4,1:T(8,128)} async-done(((f32[2,3,3,32,4,32]{3,5,0,2,4,1:T(8,128)}), f32[2,3,3,32,4,32]{3,5,0,2,4,1:T(8,128)}) %all-reduce.4.cloned.1.call-update) | async-done | bytes 294928 | tf_op jit(solution)/shard_map/psum | solution.py:288
  133.7 1.4 multiply_reduce_fusion
  135.1 0.5 mul.28
  135.6 0.3 divide_subtract_fusion
  135.9 0.2 fusion
  136.1 0.7 copy.19
  136.8 0.7 copy.18
  137.5 0.7 copy.23
  (12 shorter events, 0.1 us)
Async XLA Ops:
  7.2 2.5 %copy-start.3 = (f32[27,1024]{1,0:T(8,128)S(1)}, f32[27,1024]{1,0:T(8,128)}, u32[]{:S(2)}) copy-start(f32[27,1024]{1,0:T(8,128)} %param.7) | copy-start | bytes 331780
  7.2 126.6 %all-reduce.4.cloned.1.call-start = ((), (), s32[]{:S(2)}) async-start(), calls=%async_computation | async-start | bytes 2359296 | tf_op jit(solution)/shard_map/psum | solution.py:288
  9.7 1.6 %copy-start = (bf16[4,64,512]{2,1,0:T(8,128)(2,1)S(1)}, bf16[4,64,512]{2,1,0:T(8,128)(2,1)}, u32[]{:S(2)}) copy-start(bf16[4,64,512]{2,1,0:T(8,128)(2,1)} %v_ref.1) | copy-start | bytes 786436
  9.7 1.6 %copy-start.1 = (bf16[4,64,512]{2,1,0:T(8,128)(2,1)S(1)}, bf16[4,64,512]{2,1,0:T(8,128)(2,1)}, u32[]{:S(2)}) copy-start(bf16[4,64,512]{2,1,0:T(8,128)(2,1)} %g_ref.1) | copy-start | bytes 786436
  40.4 0.9 copy-start.2
Sparse Core Ops, SparseCore 0:
  40.6 93.1 all-reduce.3
where the time goes:
time: 145 us
  waiting for transfers between devices  91.6 us (63%)
  Pallas kernels  27.2 us (19%)
  between operations  14.9 us (10%)
  local copies, waits for them, and re-layouts  8.67 us (6%)
  other arithmetic  2.64 us (2%)
    psum x1, waiting for transfers between devices, per_device(): totals = lax.psum(sums, ('ha', 'wa'))  91.6 us
    pallas_call x1, Pallas kernels, per_device(): pl.pallas_call(functools.partial(kernel, lax.axis_size('ha'), lax.axis_si...  27.2 us
    unnamed x11, local copies, waits for them, and re-layouts  2.95 us
  transfers between devices with their start and end apart: 1, of which 1 were waited for; matrix products, arithmetic and copies ran while one was open for 0% of the time, Pallas kernels for 0%

commit v1 on v0

--- a/solution.py
+++ b/solution.py
@@ -17,8 +17,9 @@
 
 
 def kernel(
-    high, wide, v_ref, g_ref, k_ref, out_ref, sums_ref,
-    band, px, own, edge, row_in, edge_in, slope_one, gt, send_sem, recv_sem,
+    high, wide, v_ref, g_ref, k_ref, f1_ref, f2_ref, step_ref, out_ref, new1_ref, new2_ref,
+    band, px, own, edge, row_in, edge_in, slope_one, gt, part_ref, wa_in, ha_in, held, full, turned_ref,
+    send_sem, recv_sem, wa_send, wa_recv, ha_send, ha_recv,
 ):
     rows, cols, lanes = v_ref.shape
     cells = rows * cols
@@ -89,6 +90,12 @@
                 @pl.when(has(d))
                 def _():
                     copy_of(k, d).wait_send()
+        for f in range(2):
+            for stage in range(2):
+                for j in range(1, wide):
+                    wa_copy(f, stage, j).wait_send()
+                for j in range(1, high):
+                    ha_copy(f, stage, j).wait_send()
 
     col = lax.broadcasted_iota(jnp.int32, (cols, lanes), 0)
 
@@ -154,7 +161,94 @@
                     part = part + pltpu.roll(part, 64, 1)
                     part = part + pltpu.roll(part, 32, 1)
                     result = jnp.where(group == b, part, result)
-                sums_ref[f, a, c * C : (c + 1) * C, :] = result
+                at = (a * 3 + c) * C
+                part_ref[f, at : at + C, :] = result
+
+    piece = part_ref.shape[1] // (high * wide)
+    stripe = high * piece
+
+    def wa_copy(f, stage, j, arriving=False):
+        peer = lax.rem(iw + (wide - j if arriving else j), wide)
+        if stage == 0:
+            source = part_ref.at[f, pl.ds(pl.multiple_of(peer * stripe, 8), stripe)]
+            landed = wa_in.at[f, j - 1]
+            if arriving:
+                source = landed
+        else:
+            at = peer if arriving else iw
+            source = landed = full.at[f, pl.ds(pl.multiple_of(at * stripe, 8), stripe)]
+        return pltpu.make_async_remote_copy(
+            src_ref=source, dst_ref=landed,
+            send_sem=wa_send.at[f, stage, j - 1], recv_sem=wa_recv.at[f, stage, j - 1],
+            device_id={"wa": peer}, device_id_type=MESH,
+        )
+
+    def ha_copy(f, stage, j, arriving=False):
+        peer = lax.rem(ih + (high - j if arriving else j), high)
+        if stage == 0:
+            source = held.at[f, pl.ds(pl.multiple_of(peer * piece, 8), piece)]
+            landed = ha_in.at[f, j - 1]
+            if arriving:
+                source = landed
+        else:
+            at = iw * stripe + (peer if arriving else ih) * piece
+            source = landed = full.at[f, pl.ds(pl.multiple_of(at, 8), piece)]
+        return pltpu.make_async_remote_copy(
+            src_ref=source, dst_ref=landed,
+            send_sem=ha_send.at[f, stage, j - 1], recv_sem=ha_recv.at[f, stage, j - 1],
+            device_id={"ha": peer}, device_id_type=MESH,
+        )
+
+    def scatter_wa(f):
+        for j in range(1, wide):
+            wa_copy(f, 0, j).start()
+
+    def scatter_ha(f):
+        for j in range(1, wide):
+            wa_copy(f, 0, j, True).wait_recv()
+        total = part_ref[f, pl.ds(pl.multiple_of(iw * stripe, 8), stripe), :]
+        for j in range(1, wide):
+            total = total + wa_in[f, j - 1]
+        held[f] = total
+        for j in range(1, high):
+            ha_copy(f, 0, j).start()
+
+    def gather_ha(f):
+        for j in range(1, high):
+            ha_copy(f, 0, j, True).wait_recv()
+        total = held[f, pl.ds(pl.multiple_of(ih * piece, 8), piece), :]
+        for j in range(1, high):
+            total = total + ha_in[f, j - 1]
+        full[f, pl.ds(pl.multiple_of(iw * stripe + ih * piece, 8), piece), :] = total
+        for j in range(1, high):
+            ha_copy(f, 1, j).start()
+
+    def gather_wa(f):
+        for j in range(1, high):
+            ha_copy(f, 1, j, True).wait_recv()
+        for j in range(1, wide):
+            wa_copy(f, 1, j).start()
+
+    def update(f, filter_ref, new_ref):
+        for j in range(1, wide):
+            wa_copy(f, 1, j, True).wait_recv()
+        total = full[f, 0 : 9 * C, :]
+        mean = jnp.sum(total * total) / (27.0 * C * C)
+        factor = step_ref[0] * lax.rsqrt(jnp.full((C, 128), mean + 1e-06, f32))
+        for a in range(3):
+            for c in range(3):
+                at = (a * 3 + c) * C
+                flat = (total[at : at + C, :] * factor).T
+                for b in range(3):
+                    to = (a * 9 + b * 3 + c) * C
+                    turned_ref[f, to : to + C, 0:C] = flat[b * C : (b + 1) * C, :]
+        group = lax.broadcasted_iota(jnp.int32, (27, 128), 1) // C
+        for j in range(C // 4):
+            wanted = jnp.zeros((27, 128), f32)
+            for t in range(4):
+                got = turned_ref[f, pl.ds(4 * j + t, 27, stride=C), :]
+                wanted = jnp.where(group == t, pltpu.roll(got, t * C, 1) if t else got, wanted)
+            new_ref[:, j * 128 : (j + 1) * 128] = filter_ref[:, j * 128 : (j + 1) * 128] - wanted
 
     def build(f):
         lane = lax.broadcasted_iota(jnp.int32, (C, 128), 1)
@@ -190,13 +284,23 @@
         return small, SLOPE + (1.0 - SLOPE) * jnp.where(values >= 0, share, small * share)
 
     barrier = pltpu.get_barrier_semaphore()
-    for d in range(8):
+    for d in range(4, 8):
         @pl.when(has(d))
         def _():
             pl.semaphore_signal(barrier, inc=1, device_id=target(d), device_id_type=MESH)
+    for j in range(1, wide):
+        pl.semaphore_signal(
+            barrier, inc=1, device_id={"wa": lax.rem(iw + j, wide)}, device_id_type=MESH
+        )
+    for j in range(1, high):
+        pl.semaphore_signal(
+            barrier, inc=1, device_id={"ha": lax.rem(ih + j, high)}, device_id_type=MESH
+        )
 
     edge[...] = jnp.zeros(edge.shape, f32)
     gt[...] = jnp.zeros(gt.shape, bf16)
+    turned_ref[...] = jnp.zeros(turned_ref.shape, f32)
+    part_ref[:, 9 * C :, :] = jnp.zeros((2, part_ref.shape[1] - 9 * C, 128), f32)
     for d in range(8):
         @pl.when(jnp.logical_not(has(d)))
         def _():
@@ -207,9 +311,9 @@
                     edge_in[k, d - 2] = jnp.zeros(edge.shape[2:], f32)
     volume = v_ref[...].astype(f32)
     set_edges(0, volume)
-    tall = 1 + jnp.where(ih > 0, 1, 0) + jnp.where(ih < high - 1, 1, 0)
-    broad = 1 + jnp.where(iw > 0, 1, 0) + jnp.where(iw < wide - 1, 1, 0)
-    pl.semaphore_wait(barrier, tall * broad - 1)
+    tall = jnp.where(ih > 0, 1, 0) + jnp.where(ih < high - 1, 1, 0)
+    broad = jnp.where(iw > 0, 1, 0) + jnp.where(iw < wide - 1, 1, 0)
+    pl.semaphore_wait(barrier, tall * broad + wide + high - 2)
     send(0)
     build(0)
     build(1)
@@ -233,6 +337,7 @@
     set_edges(2, own[1].astype(f32))
     send(2)
     filter_sums(1, 1, own[1].astype(f32).reshape(cells, lanes))
+    scatter_wa(1)
     receive(2)
     assemble(2, own[1].astype(f32))
 
@@ -240,11 +345,19 @@
     own[2] = grad.reshape(rows, cols, lanes)
     set_edges(3, own[2].astype(f32))
     send(3)
+    scatter_ha(1)
     filter_sums(0, 0, own[2].astype(f32).reshape(cells, lanes))
+    scatter_wa(0)
+    gather_ha(1)
     receive(3)
     assemble(3, own[2].astype(f32))
-
+    scatter_ha(0)
+    gather_wa(1)
     out_ref[...] = conv_back(3, 0).astype(bf16).reshape(rows, cols, lanes)
+    gather_ha(0)
+    update(1, f2_ref, new2_ref)
+    gather_wa(0)
+    update(0, f1_ref, new1_ref)
     finish()
 
 
@@ -260,15 +373,18 @@
     )
     rows, cols, lanes = volume.shape
     tall = -(-rows // 8) * 8
+    high, wide = lax.axis_size("ha"), lax.axis_size("wa")
+    piece = -(-9 * C // (high * wide * 8)) * 8
     vmem = pl.BlockSpec(memory_space=pltpu.VMEM)
-    grad_input, sums = pl.pallas_call(
-        functools.partial(kernel, lax.axis_size("ha"), lax.axis_size("wa")),
+    return pl.pallas_call(
+        functools.partial(kernel, high, wide),
         out_shape=(
             jax.ShapeDtypeStruct(volume.shape, jnp.bfloat16),
-            jax.ShapeDtypeStruct((2, 3, 3 * C, 128), jnp.float32),
+            jax.ShapeDtypeStruct(filter_one.shape, jnp.float32),
+            jax.ShapeDtypeStruct(filter_two.shape, jnp.float32),
         ),
-        in_specs=[vmem] * 3,
-        out_specs=(vmem, vmem),
+        in_specs=[vmem] * 5 + [pl.BlockSpec(memory_space=pltpu.SMEM)],
+        out_specs=(vmem,) * 3,
         scratch_shapes=[
             pltpu.VMEM((2, 3, 3 * lanes, lanes), jnp.bfloat16),
             pltpu.VMEM((4, rows + 2, cols, 3 * lanes), jnp.bfloat16),
@@ -278,23 +394,23 @@
             pltpu.VMEM((4, 6, tall, lanes), jnp.float32),
             pltpu.VMEM((rows * cols, lanes), jnp.float32),
             pltpu.VMEM((lanes + 2 * C, rows * cols), jnp.bfloat16),
+            pltpu.VMEM((2, high * wide * piece, 128), jnp.float32),
+            pltpu.VMEM((2, wide - 1, high * piece, 128), jnp.float32),
+            pltpu.VMEM((2, high - 1, piece, 128), jnp.float32),
+            pltpu.VMEM((2, high * piece, 128), jnp.float32),
+            pltpu.VMEM((2, high * wide * piece, 128), jnp.float32),
+            pltpu.VMEM((2, 27 * C, 128), jnp.float32),
             pltpu.SemaphoreType.DMA((4, 8)),
             pltpu.SemaphoreType.DMA((4, 8)),
+            pltpu.SemaphoreType.DMA((2, 2, wide - 1)),
+            pltpu.SemaphoreType.DMA((2, 2, wide - 1)),
+            pltpu.SemaphoreType.DMA((2, 2, high - 1)),
+            pltpu.SemaphoreType.DMA((2, 2, high - 1)),
         ],
         compiler_params=pltpu.CompilerParams(
             collective_id=0, has_side_effects=True, vmem_limit_bytes=44 * 2**20
         ),
-    )(volume, grad_out, kernels)
-    totals = lax.psum(sums, ("ha", "wa"))
-    totals = (
-        totals.reshape(2, 3, 3, C, 4, C)[:, :, :, :, :3]
-        .transpose(0, 1, 4, 2, 5, 3)
-        .reshape(2, 27, C * C)
-    )
-    filters = jnp.stack([filter_one, filter_two])
-    spread = jnp.sqrt(jnp.mean(totals * totals, axis=(1, 2)) + 1e-06)
-    result = filters - step_size[0] * totals / spread[:, None, None]
-    return (grad_input, result[0], result[1])
+    )(volume, grad_out, kernels, filter_one, filter_two, step_size)
 
 
 def solution(mesh):

time: 145 us -> 49.2 us (0.34)
  waiting for transfers between devices: 91.6 us -> 0 us
  Pallas kernels: 27.2 us -> 40.7 us
  between operations: 14.9 us -> 1.45 us
  local copies, waits for them, and re-layouts: 8.67 us -> 5.94 us
  other arithmetic: 2.64 us -> 0.95 us
    psum x1 -> x0, waiting for transfers between devices: 91.6 us -> none  [per_device(): totals = lax.psum(sums, ('ha', 'wa'))]
    pallas_call x1, Pallas kernels: 27.2 us -> 40.7 us  [per_device(): pl.pallas_call(functools.partial(kernel, high, wide), out_shape=(jax.Shap...]
    reshape x2 -> x0, local copies, waits for them, and re-layouts: 1.89 us -> none  [per_device(): totals.reshape(2, 3, 3, C, 4, C)[:, :, :, :, :3].transpose(0, 1, 4, 2, 5, 3)]
  transfers between devices with their start and end apart: 1 -> 0, of which waited for: 1 -> 0; matrix products, arithmetic and copies ran while one was open for 0% -> 0% of each run, Pallas kernels for 0% -> 0%
where the time goes in v1:
time: 49.2 us; the launch traced here: 49 us
  Pallas kernels  40.7 us (83%)
  local copies, waits for them, and re-layouts  5.94 us (12%)
  between operations  1.45 us (3%)
  other arithmetic  0.95 us (2%)
    pallas_call x1, Pallas kernels, per_device(): pl.pallas_call(functools.partial(kernel, high, wide), out_shape=(jax.Shap...  40.7 us
    unnamed x11, local copies, waits for them, and re-layouts  2.95 us
    rev x2, local copies, waits for them, and re-layouts, strips(): kernel_one.reshape(9, 3, C, C)[:, ::-1].transpose(0, 2, 1, 3)  1.96 us
    reshape x6, local copies, waits for them, and re-layouts, strips(): kernel_one.reshape(9, 3, C, C)[:, ::-1].transpose(0, 2, 1, 3)  0.99 us

profile of v1, /device:TPU:0, one launch (start us, length us, event | category | flops | bytes accessed | tf_op | source)
XLA Modules:
  0.0 49.0 jit_solution(11833876750615001403)
XLA Ops:
  0.6 0.0 copy-start
  1.3 0.9 %multiply_convert_fusion.1 = bf16[27,1024]{1,0:T(8,128)(2,1)S(1)} fusion(f32[27,1024]{1,0:T(8,128)} %f1_ref.1), kind=kLoop, calls=%fused_computation.2 | loop fusion | flops 55296 | bytes 165888 | tf_op jit(solution)/shard_map/convert_element_type | solution.py:372
  2.2 0.0 copy-done
  2.3 0.2 reshape.20
  2.5 0.2 copy.11
  2.6 1.0 %rev.7 = bf16[9,3,32,32]{3,1,2,0:T(4,128)(2,1)S(1)} reverse(bf16[9,3,32,32]{3,1,2,0:T(4,128)(2,1)S(1)} %copy.11), dimensions={1} | reverse | bytes 110592 | tf_op jit(solution)/shard_map/rev | solution.py:365
  3.6 0.2 reshape.21
  3.8 0.2 reshape.18
  4.0 0.2 copy.10
  4.1 1.0 %rev.6 = bf16[9,3,32,32]{3,1,2,0:T(4,128)(2,1)S(1)} reverse(bf16[9,3,32,32]{3,1,2,0:T(4,128)(2,1)S(1)} %copy.10), dimensions={1} | reverse | bytes 110592 | tf_op jit(solution)/shard_map/rev | solution.py:365
  5.1 0.0 copy-start.3
  5.1 0.2 reshape.19
  5.3 0.0 copy-start.2
  5.4 0.0 copy-start.1
  5.4 0.7 %copy-done.3 = bf16[4,64,512]{2,1,0:T(8,128)(2,1)S(1)} copy-done((bf16[4,64,512]{2,1,0:T(8,128)(2,1)S(1)}, bf16[4,64,512]{2,1,0:T(8,128)(2,1)}, u32[]{:S(2)}) %copy-start.3) | copy-done | bytes 262168
  6.1 0.2 copy-done.2
  6.3 0.0 copy-done.1
  6.3 40.7 %shard_map.76 = (bf16[4,64,512]{2,1,0:T(8,128)(2,1)S(1)}, f32[27,1024]{1,0:T(8,128)S(1)}, f32[27,1024]{1,0:T(8,128)S(1)}) custom-call(bf16[4,64,512]{2,1,0:T(8,128)(2,1)S(1)} %copy-done.2, bf16[4,64,512]{2,1,0:T(8,128)(2,1)S(1)} %copy-done.3, bf16[2,9,32,128]{3,2,1,0:T(8,128)(2,1)S(1)} %pad_maximum_fusion.k_ref, f32[27,1024]{1,0:T(8,128)S(1)} %copy-done.1, ...), custom_call_target="tpu_custom_call" | custom-call | tf_op jit(solution)/shard_map/pallas_call | solution.py:379
  47.0 0.7 %copy.16 = bf16[4,64,512]{2,1,0:T(8,128)(2,1)} copy(bf16[4,64,512]{2,1,0:T(8,128)(2,1)S(1)} %get-tuple-element.8) | data formatting | bytes 524288
  47.7 0.7 %copy.17 = f32[27,1024]{1,0:T(8,128)} copy(f32[27,1024]{1,0:T(8,128)S(1)} %get-tuple-element.9) | data formatting | bytes 221184
  48.4 0.7 %copy.18 = f32[27,1024]{1,0:T(8,128)} copy(f32[27,1024]{1,0:T(8,128)S(1)} %get-tuple-element.10) | data formatting | bytes 221184
  (3 shorter events, 0.1 us)
Async XLA Ops:
  0.6 1.6 %copy-start = (f32[27,1024]{1,0:T(8,128)S(1)}, f32[27,1024]{1,0:T(8,128)}, u32[]{:S(2)}) copy-start(f32[27,1024]{1,0:T(8,128)} %f2_ref.1) | copy-start | bytes 331780
  5.1 1.0 %copy-start.3 = (bf16[4,64,512]{2,1,0:T(8,128)(2,1)S(1)}, bf16[4,64,512]{2,1,0:T(8,128)(2,1)}, u32[]{:S(2)}) copy-start(bf16[4,64,512]{2,1,0:T(8,128)(2,1)} %g_ref.1) | copy-start | bytes 786436
  5.3 1.0 %copy-start.2 = (bf16[4,64,512]{2,1,0:T(8,128)(2,1)S(1)}, bf16[4,64,512]{2,1,0:T(8,128)(2,1)}, u32[]{:S(2)}) copy-start(bf16[4,64,512]{2,1,0:T(8,128)(2,1)} %v_ref.1) | copy-start | bytes 786436
  5.4 1.0 %copy-start.1 = (f32[27,1024]{1,0:T(8,128)S(1)}, f32[27,1024]{1,0:T(8,128)}, u32[]{:S(2)}) copy-start(f32[27,1024]{1,0:T(8,128)} %f1_ref.1) | copy-start | bytes 331780

commit v2 on v1

--- a/solution.py
+++ b/solution.py
@@ -17,9 +17,10 @@
 
 
 def kernel(
-    high, wide, v_ref, g_ref, k_ref, f1_ref, f2_ref, step_ref, out_ref, new1_ref, new2_ref,
+    high, wide, v_any, g_any, f1_any, f2_any, step_ref, out_ref, new1_ref, new2_ref,
     band, px, own, edge, row_in, edge_in, slope_one, gt, part_ref, wa_in, ha_in, held, full, turned_ref,
-    send_sem, recv_sem, wa_send, wa_recv, ha_send, ha_recv,
+    v_ref, g_ref, f1_ref, f2_ref,
+    send_sem, recv_sem, wa_send, wa_recv, ha_send, ha_recv, load_sem,
 ):
     rows, cols, lanes = v_ref.shape
     cells = rows * cols
@@ -115,22 +116,11 @@
         put_row(k, rows + 1, row_in[k, 1].astype(f32),
                 edge_in[k, 4, 0:1, :], edge_in[k, 5, 0:1, :])
 
-    def conv(k, f):
+    def conv(k, f, heights=(0, 1, 2)):
         total = jnp.zeros((cells, lanes), f32)
-        for a in range(3):
+        for a in heights:
             left = px[k, a : a + rows].reshape(cells, 3 * lanes)
             total += jnp.dot(left, band[f, a], preferred_element_type=f32)
-        return total
-
-    def conv_back(k, f):
-        total = jnp.zeros((cells, lanes), f32)
-        for a in range(3):
-            for b in range(3):
-                left = px[k, a : a + rows, :, b * lanes : (b + 1) * lanes].reshape(cells, lanes)
-                right = band[f, 2 - a, (2 - b) * lanes : (3 - b) * lanes, :]
-                total += lax.dot_general(
-                    left, right, (((1,), (1,)), ((), ())), preferred_element_type=f32
-                )
         return total
 
     def filter_sums(k, f, grad):
@@ -250,12 +240,43 @@
                 wanted = jnp.where(group == t, pltpu.roll(got, t * C, 1) if t else got, wanted)
             new_ref[:, j * 128 : (j + 1) * 128] = filter_ref[:, j * 128 : (j + 1) * 128] - wanted
 
-    def build(f):
+    def spread(f, filter_ref):
+        scaled = (filter_ref[...] * (1.0 / math.sqrt(27.0 * C))).astype(bf16).astype(f32)
+        for j in range(C // 4):
+            tile = scaled[:, j * 128 : (j + 1) * 128]
+            for t in range(4):
+                turned_ref[f, pl.ds(4 * j + t, 27, stride=C), :] = (
+                    pltpu.roll(tile, 128 - t * C, 1) if t else tile
+                )
+
+    def strip_of(f, a, b, back):
+        group = lax.broadcasted_iota(jnp.int32, (C, 128), 1) // C
+        blocks = []
+        for c in range(3):
+            at = (a * 9 + b * 3 + c) * C
+            blocks.append(turned_ref[f, at : at + C, :])
+        if back:
+            blocks = [blocks[0], pltpu.roll(blocks[1], C, 1), pltpu.roll(blocks[2], 2 * C, 1)]
+        else:
+            blocks = [blocks[2], pltpu.roll(blocks[1], C, 1), pltpu.roll(blocks[0], 2 * C, 1)]
+        strip = jnp.zeros((C, 128), f32)
+        for c in range(3):
+            strip = jnp.where(group == c, blocks[c], strip)
+        if not back:
+            return strip
+        flat = jnp.concatenate([strip] * 4, axis=0).T
+        strip = jnp.zeros((C, 128), f32)
+        for c in range(3):
+            strip = jnp.where(group == c, flat[c * C : (c + 1) * C, :], strip)
+        return strip
+
+    def build(f, back):
+        m = f + 2 * back
         lane = lax.broadcasted_iota(jnp.int32, (C, 128), 1)
         zero = jnp.zeros((C, 128), f32)
         for a in range(3):
             for b in range(3):
-                strip = k_ref[f, a * 3 + b].astype(f32)
+                strip = strip_of(f, 2 - a if back else a, 2 - b if back else b, back)
                 turned = [
                     pltpu.roll(strip, 96, 1), strip, pltpu.roll(strip, 32, 1), pltpu.roll(strip, 64, 1)
                 ]
@@ -276,13 +297,21 @@
                         at = b * lanes + q * 128 + s * C
                         for t in range(tiles):
                             block = {-1: low, 0: middle, 1: high_part}.get(t - q, none)
-                            band[f, a, at : at + C, t * 128 : (t + 1) * 128] = block
+                            band[m, a, at : at + C, t * 128 : (t + 1) * 128] = block
 
     def sharing(values):
         small = jnp.exp(-jnp.abs(values))
         share = 1.0 / (1.0 + small)
         return small, SLOPE + (1.0 - SLOPE) * jnp.where(values >= 0, share, small * share)
 
+    loads = [
+        pltpu.make_async_copy(source, landed, load_sem.at[n])
+        for n, (source, landed) in enumerate(
+            ((v_any, v_ref), (f1_any, f1_ref), (f2_any, f2_ref), (g_any, g_ref))
+        )
+    ]
+    for load in loads:
+        load.start()
     barrier = pltpu.get_barrier_semaphore()
     for d in range(4, 8):
         @pl.when(has(d))
@@ -299,7 +328,6 @@
 
     edge[...] = jnp.zeros(edge.shape, f32)
     gt[...] = jnp.zeros(gt.shape, bf16)
-    turned_ref[...] = jnp.zeros(turned_ref.shape, f32)
     part_ref[:, 9 * C :, :] = jnp.zeros((2, part_ref.shape[1] - 9 * C, 128), f32)
     for d in range(8):
         @pl.when(jnp.logical_not(has(d)))
@@ -309,14 +337,16 @@
                     row_in[k, d] = jnp.zeros((cols, lanes), bf16)
                 else:
                     edge_in[k, d - 2] = jnp.zeros(edge.shape[2:], f32)
+    loads[0].wait()
     volume = v_ref[...].astype(f32)
     set_edges(0, volume)
     tall = jnp.where(ih > 0, 1, 0) + jnp.where(ih < high - 1, 1, 0)
     broad = jnp.where(iw > 0, 1, 0) + jnp.where(iw < wide - 1, 1, 0)
     pl.semaphore_wait(barrier, tall * broad + wide + high - 2)
     send(0)
-    build(0)
-    build(1)
+    loads[1].wait()
+    spread(0, f1_ref)
+    build(0, 0)
     receive(0)
     assemble(0, v_ref[...].astype(f32))
 
@@ -328,23 +358,29 @@
     own[0] = act
     set_edges(1, act.astype(f32))
     send(1)
+    loads[2].wait()
+    spread(1, f2_ref)
+    build(1, 0)
     receive(1)
     assemble(1, own[0].astype(f32))
 
+    loads[3].wait()
     slope = sharing(conv(1, 1))[1]
     grad = (g_ref[...].astype(f32).reshape(cells, lanes) * slope).astype(bf16)
     own[1] = grad.reshape(rows, cols, lanes)
     set_edges(2, own[1].astype(f32))
     send(2)
+    build(1, 1)
     filter_sums(1, 1, own[1].astype(f32).reshape(cells, lanes))
     scatter_wa(1)
     receive(2)
     assemble(2, own[1].astype(f32))
 
-    grad = (conv_back(2, 1) * slope_one[...]).astype(bf16)
+    grad = (conv(2, 3) * slope_one[...]).astype(bf16)
     own[2] = grad.reshape(rows, cols, lanes)
     set_edges(3, own[2].astype(f32))
     send(3)
+    build(0, 1)
     scatter_ha(1)
     filter_sums(0, 0, own[2].astype(f32).reshape(cells, lanes))
     scatter_wa(0)
@@ -353,24 +389,16 @@
     assemble(3, own[2].astype(f32))
     scatter_ha(0)
     gather_wa(1)
-    out_ref[...] = conv_back(3, 0).astype(bf16).reshape(rows, cols, lanes)
+    early = conv(3, 2, (0, 1))
     gather_ha(0)
+    out_ref[...] = (early + conv(3, 2, (2,))).astype(bf16).reshape(rows, cols, lanes)
+    gather_wa(0)
     update(1, f2_ref, new2_ref)
-    gather_wa(0)
     update(0, f1_ref, new1_ref)
     finish()
 
 
-def strips(kernel_one):
-    parts = kernel_one.reshape(9, 3, C, C)[:, ::-1].transpose(0, 2, 1, 3).reshape(9, C, 3 * C)
-    return jnp.pad(parts, ((0, 0), (0, 0), (0, C)))
-
-
 def per_device(volume, grad_out, filter_one, filter_two, step_size):
-    scale = 1.0 / math.sqrt(27.0 * C)
-    kernels = jnp.stack(
-        [strips((f * scale).astype(jnp.bfloat16)) for f in (filter_one, filter_two)]
-    )
     rows, cols, lanes = volume.shape
     tall = -(-rows // 8) * 8
     high, wide = lax.axis_size("ha"), lax.axis_size("wa")
@@ -383,10 +411,10 @@
             jax.ShapeDtypeStruct(filter_one.shape, jnp.float32),
             jax.ShapeDtypeStruct(filter_two.shape, jnp.float32),
         ),
-        in_specs=[vmem] * 5 + [pl.BlockSpec(memory_space=pltpu.SMEM)],
+        in_specs=[pl.BlockSpec(memory_space=pl.ANY)] * 4 + [pl.BlockSpec(memory_space=pltpu.SMEM)],
         out_specs=(vmem,) * 3,
         scratch_shapes=[
-            pltpu.VMEM((2, 3, 3 * lanes, lanes), jnp.bfloat16),
+            pltpu.VMEM((4, 3, 3 * lanes, lanes), jnp.bfloat16),
             pltpu.VMEM((4, rows + 2, cols, 3 * lanes), jnp.bfloat16),
             pltpu.VMEM((3, rows, cols, lanes), jnp.bfloat16),
             pltpu.VMEM((4, 2, tall, lanes), jnp.float32),
@@ -400,17 +428,22 @@
             pltpu.VMEM((2, high * piece, 128), jnp.float32),
             pltpu.VMEM((2, high * wide * piece, 128), jnp.float32),
             pltpu.VMEM((2, 27 * C, 128), jnp.float32),
+            pltpu.VMEM(volume.shape, volume.dtype),
+            pltpu.VMEM(grad_out.shape, grad_out.dtype),
+            pltpu.VMEM(filter_one.shape, filter_one.dtype),
+            pltpu.VMEM(filter_two.shape, filter_two.dtype),
             pltpu.SemaphoreType.DMA((4, 8)),
             pltpu.SemaphoreType.DMA((4, 8)),
             pltpu.SemaphoreType.DMA((2, 2, wide - 1)),
             pltpu.SemaphoreType.DMA((2, 2, wide - 1)),
             pltpu.SemaphoreType.DMA((2, 2, high - 1)),
             pltpu.SemaphoreType.DMA((2, 2, high - 1)),
+            pltpu.SemaphoreType.DMA((4,)),
         ],
         compiler_params=pltpu.CompilerParams(
-            collective_id=0, has_side_effects=True, vmem_limit_bytes=44 * 2**20
+            collective_id=0, has_side_effects=True, vmem_limit_bytes=63 * 2**20
         ),
-    )(volume, grad_out, kernels, filter_one, filter_two, step_size)
+    )(volume, grad_out, filter_one, filter_two, step_size)
 
 
 def solution(mesh):

time: 49.2 us -> 46.2 us (0.939)
  local copies, waits for them, and re-layouts: 5.94 us -> 3.31 us
  other arithmetic: 0.95 us -> 0 us
  Pallas kernels: 40.7 us -> 41.4 us
    rev x2 -> x0, local copies, waits for them, and re-layouts: 1.96 us -> none  [strips(): kernel_one.reshape(9, 3, C, C)[:, ::-1].transpose(0, 2, 1, 3)]
    reshape x6 -> x0, local copies, waits for them, and re-layouts: 0.99 us -> none  [strips(): kernel_one.reshape(9, 3, C, C)[:, ::-1].transpose(0, 2, 1, 3)]
    convert_element_type x2 -> x0, other arithmetic: 0.93 us -> none  [per_device(): (f * scale).astype(jnp.bfloat16)]
    pallas_call x1, Pallas kernels: 40.7 us -> 41.4 us  [per_device(): pl.pallas_call(functools.partial(kernel, high, wide), out_shape=(jax.Shap...]
    unnamed x11 -> x7, local copies, waits for them, and re-layouts: 2.95 us -> 3.31 us
where the time goes in v2:
time: 46.2 us; the launch traced here: 46 us
  Pallas kernels  41.4 us (90%)
  local copies, waits for them, and re-layouts  3.31 us (7%)
  between operations  1.3 us (3%)
    pallas_call x1, Pallas kernels, per_device(): pl.pallas_call(functools.partial(kernel, high, wide), out_shape=(jax.Shap...  41.4 us
    unnamed x7, local copies, waits for them, and re-layouts  3.31 us

profile of v2, /device:TPU:0, one launch (start us, length us, event | category | flops | bytes accessed | tf_op | source)
XLA Modules:
  0.0 46.0 jit_solution(8564843006352111802)
XLA Ops:
  1.3 41.4 %shard_map.76 = (bf16[4,64,512]{2,1,0:T(8,128)(2,1)}, f32[27,1024]{1,0:T(8,128)}, f32[27,1024]{1,0:T(8,128)}) custom-call(bf16[4,64,512]{2,1,0:T(8,128)(2,1)} %v_any.1, bf16[4,64,512]{2,1,0:T(8,128)(2,1)} %g_any.1, f32[27,1024]{1,0:T(8,128)} %f1_any.1, f32[27,1024]{1,0:T(8,128)} %f2_any.1, f32[1]{0:T(128)S(6)} %copy.11.step_ref), custom_call_target="tpu_custom_call" | custom-call | tf_op jit(solution)/shard_map/pallas_call | solution.py:407
  42.6 0.0 copy-start.1
  42.7 1.7 %copy.12 = bf16[4,64,512]{2,1,0:T(8,128)(2,1)} copy(bf16[4,64,512]{2,1,0:T(8,128)(2,1)} %get-tuple-element.6) | data formatting | bytes 524288
  44.4 0.0 copy-done.1
  44.4 0.0 copy-start
  44.4 0.7 %copy.13 = f32[27,1024]{1,0:T(8,128)} copy(f32[27,1024]{1,0:T(8,128)S(1)} %copy-done.1) | data formatting | bytes 221184
  45.0 0.3 copy-done
  45.3 0.7 %copy.14 = f32[27,1024]{1,0:T(8,128)} copy(f32[27,1024]{1,0:T(8,128)S(1)} %copy-done) | data formatting | bytes 221184
Async XLA Ops:
  42.6 1.7 %copy-start.1 = (f32[27,1024]{1,0:T(8,128)S(1)}, f32[27,1024]{1,0:T(8,128)}, u32[]{:S(2)}) copy-start(f32[27,1024]{1,0:T(8,128)} %get-tuple-element.7) | copy-start | bytes 331780
  44.4 1.0 %copy-start = (f32[27,1024]{1,0:T(8,128)S(1)}, f32[27,1024]{1,0:T(8,128)}, u32[]{:S(2)}) copy-start(f32[27,1024]{1,0:T(8,128)} %get-tuple-element.8) | copy-start | bytes 331780
